TPU v7x, 32 devices: a whole 2x2x4 slice. The times are simulated.
32 devices in a mesh: dp: 8 (over z, x), seq: 4 (over y, core).
Axes of the slice: x: 2, y: 2, z: 4, core: 2. Of those that a mesh axis runs over, the one named last changes fastest.
Arguments:
- hidden_in: bfloat16 [24576, 1024], P(('dp', 'seq')), may hold values from -6 to 6
- key_bias: float32 [8, 3072], P('dp', 'seq'), may hold values from -4 to 4
- w_qkv: bfloat16 [1024, 3072], P('dp'), may hold values from -0.1875 to 0.1875
- bias_q: bfloat16 [1024], P('dp'), may hold values from -3 to 3
- bias_v: bfloat16 [1024], P('dp'), may hold values from -0.75 to 0.75
- w_out: bfloat16 [1024, 1024], P('dp'), may hold values from -3 to 3
- bias_out: bfloat16 [1024], P('dp'), may hold values from -3 to 3
- gain_attn: bfloat16 [1024], P('dp'), may hold values from 0.25 to 1.75
- shift_attn: bfloat16 [1024], P('dp'), may hold values from -3 to 3
- w_up: bfloat16 [1024, 4096], P('dp'), may hold values from -0.1875 to 0.1875
- bias_up: bfloat16 [4096], P('dp'), may hold values from -3 to 3
- w_down: bfloat16 [4096, 1024], P('dp'), may hold values from -0.09375 to 0.09375
- bias_down: bfloat16 [1024], P('dp'), may hold values from -3 to 3
- gain_ffn: bfloat16 [1024], P('dp'), may hold values from 0.25 to 1.75
- shift_ffn: bfloat16 [1024], P('dp'), may hold values from -3 to 3
- grad_out: bfloat16 [24576, 1024], P(('dp', 'seq')), may hold values from -6 to 6
Outputs:
- output: bfloat16 [24576, 1024], P(('dp', 'seq'))
- grad_in: float32 [24576, 1024], P(('dp', 'seq'))
- grad_w_qkv: float32 [1024, 3072], P('dp')
- grad_bias_q: float32 [1024], P('dp')
- grad_bias_v: float32 [1024], P('dp')
- grad_w_out: float32 [1024, 1024], P('dp')
- grad_bias_out: float32 [1024], P('dp')
- grad_gain_attn: float32 [1024], P('dp')
- grad_shift_attn: float32 [1024], P('dp')
- grad_w_up: float32 [1024, 4096], P('dp')
- grad_bias_up: float32 [4096], P('dp')
- grad_w_down: float32 [4096, 1024], P('dp')
- grad_bias_down: float32 [1024], P('dp')
- grad_gain_ffn: float32 [1024], P('dp')
- grad_shift_ffn: float32 [1024], P('dp')
All inputs are finite; a program needn't handle non-finite values.
Results may differ from a plain program's by a relative error of at most 0.02.
Values may be sent and summed in bfloat16 or wider, within the bound.
A program may use at most 192 MiB of HBM per device.

v0:
```python
import jax
import jax.numpy as jnp
from jax import lax
from jax.sharding import PartitionSpec as P

HEAD_DIM = 64
norm_eps = 1e-05


def shortened(array):

    def short(part):
        return part.astype(jnp.bfloat16) if part.dtype == jnp.float32 else part

    return jax.tree.map(short, array)


def layer_norm(hidden, gain_vec, shift_vec):
    row_mean = jnp.mean(hidden, -1, keepdims=True)
    centered = hidden - row_mean
    row_var = jnp.mean(centered * centered, -1, keepdims=True)
    return centered * lax.rsqrt(row_var + norm_eps) * gain_vec + shift_vec


def gelu_exact(pre_act):
    return jax.nn.gelu(pre_act, approximate=False)


def matmul(left, right):
    return jnp.dot(left, right, preferred_element_type=jnp.float32)


def matmul_left(left, right):
    return lax.dot_general(
        left, right, (((0,), (0,)), ((), ())), preferred_element_type=jnp.float32
    )


def matmul_right(left, right):
    return lax.dot_general(
        left, right, (((1,), (1,)), ((), ())), preferred_element_type=jnp.float32
    )


def attend_forward(queries, keys_all, values_all, bias_row, score_scale):
    length, heads_loc, head_width = queries.shape
    block_rows = min(512, length)
    head_step = min(2, heads_loc)
    blocks = queries.reshape(length // block_rows, block_rows, heads_loc, head_width)

    def one_block(query_blk):
        pieces = []
        totals_list = []
        for start_head in range(0, heads_loc, head_step):
            part = slice(start_head, start_head + head_step)
            scores = (
                jnp.einsum(
                    "bhe,lhe->hbl",
                    query_blk[:, part],
                    keys_all[:, part],
                    preferred_element_type=jnp.float32,
                )
                * score_scale
                + bias_row
            )
            row_max = jnp.max(scores, -1, keepdims=True)
            expo = jnp.exp(scores - row_max)
            row_total = jnp.sum(expo, -1, keepdims=True)
            probs_low = (expo / row_total).astype(jnp.bfloat16)
            pieces.append(
                jnp.einsum(
                    "hbl,lhe->bhe",
                    probs_low,
                    values_all[:, part],
                    preferred_element_type=jnp.float32,
                )
            )
            totals_list.append((row_max + jnp.log(row_total))[..., 0])
        return (jnp.concatenate(pieces, 1).astype(jnp.bfloat16), jnp.concatenate(totals_list, 0))

    context, log_total = lax.map(one_block, blocks)
    return (context.reshape(length, heads_loc * head_width), log_total)


def attend_backward(queries, keys_all, values_all, bias_row, score_scale, log_total, context_grad):
    length, heads_loc, head_width = queries.shape
    block_rows = min(512, length)
    head_step = min(2, heads_loc)
    query_blocks = queries.reshape(length // block_rows, block_rows, heads_loc, head_width)
    grad_blocks = context_grad.reshape(length // block_rows, block_rows, heads_loc, head_width)

    def one_block(carry_in, item_in):
        key_acc, value_acc = carry_in
        query_blk, grad_blk, total_blk = item_in
        query_parts = []
        key_parts = []
        value_parts = []
        for start_head in range(0, heads_loc, head_step):
            part = slice(start_head, start_head + head_step)
            scores = (
                jnp.einsum(
                    "bhe,lhe->hbl",
                    query_blk[:, part],
                    keys_all[:, part],
                    preferred_element_type=jnp.float32,
                )
                * score_scale
                + bias_row
            )
            probs_full = jnp.exp(scores - total_blk[part][..., None])
            d_probs = jnp.einsum(
                "bhe,lhe->hbl",
                grad_blk[:, part],
                values_all[:, part],
                preferred_element_type=jnp.float32,
            )
            row_dot = jnp.sum(probs_full * d_probs, -1, keepdims=True)
            d_scores = (probs_full * (d_probs - row_dot)).astype(jnp.bfloat16)
            query_parts.append(
                jnp.einsum(
                    "hbl,lhe->bhe", d_scores, keys_all[:, part], preferred_element_type=jnp.float32
                )
                * score_scale
            )
            key_parts.append(
                jnp.einsum(
                    "hbl,bhe->lhe", d_scores, query_blk[:, part], preferred_element_type=jnp.float32
                )
                * score_scale
            )
            value_parts.append(
                jnp.einsum(
                    "hbl,bhe->lhe",
                    probs_full.astype(jnp.bfloat16),
                    grad_blk[:, part],
                    preferred_element_type=jnp.float32,
                )
            )
        key_acc = key_acc + jnp.concatenate(key_parts, 1)
        value_acc = value_acc + jnp.concatenate(value_parts, 1)
        return ((key_acc, value_acc), jnp.concatenate(query_parts, 1))

    empty = jnp.zeros((length, heads_loc, head_width), jnp.float32)
    (key_grad, value_grad), query_grad = lax.scan(
        one_block, (empty, empty), (query_blocks, grad_blocks, log_total)
    )
    return (query_grad.reshape(length, heads_loc, head_width), key_grad, value_grad)


def local(
    hidden_in,
    key_bias,
    w_qkv,
    bias_q,
    bias_v,
    w_out,
    bias_out,
    gain_attn,
    shift_attn,
    w_up,
    bias_up,
    w_down,
    bias_down,
    gain_ffn,
    shift_ffn,
    grad_out,
):
    groups = lax.axis_size("seq")
    params = (
        lax.all_gather(w_qkv, "dp", axis=0, tiled=True),
        lax.all_gather(bias_q, "dp", axis=0, tiled=True),
        lax.all_gather(bias_v, "dp", axis=0, tiled=True),
        lax.all_gather(w_out, "dp", axis=0, tiled=True),
        lax.all_gather(bias_out, "dp", axis=0, tiled=True),
        lax.all_gather(gain_attn, "dp", axis=0, tiled=True),
        lax.all_gather(shift_attn, "dp", axis=0, tiled=True),
        lax.all_gather(w_up, "dp", axis=0, tiled=True),
        lax.all_gather(bias_up, "dp", axis=0, tiled=True),
        lax.all_gather(w_down, "dp", axis=0, tiled=True),
        lax.all_gather(bias_down, "dp", axis=0, tiled=True),
        lax.all_gather(gain_ffn, "dp", axis=0, tiled=True),
        lax.all_gather(shift_ffn, "dp", axis=0, tiled=True),
    )
    full_bias_q = params[1].astype(jnp.float32)
    full_bias_v = params[2].astype(jnp.float32)
    full_bias_out = params[4].astype(jnp.float32)
    full_gain_attn = params[5].astype(jnp.float32)
    full_shift_attn = params[6].astype(jnp.float32)
    full_bias_up = params[8].astype(jnp.float32)
    full_bias_down = params[10].astype(jnp.float32)
    full_gain_ffn = params[11].astype(jnp.float32)
    full_shift_ffn = params[12].astype(jnp.float32)
    tok_rows, model_width = hidden_in.shape
    group_width = model_width // groups
    heads_loc = group_width // HEAD_DIM
    score_scale = HEAD_DIM ** (-0.5)
    no_bias = jnp.zeros((model_width,), jnp.float32)
    qkv_rows = matmul(hidden_in, params[0]) + jnp.concatenate([full_bias_q, no_bias, full_bias_v])
    qkv_rows = qkv_rows.astype(jnp.bfloat16).reshape(tok_rows, 3, groups, group_width)
    heads_in = lax.all_to_all(qkv_rows, "seq", split_axis=2, concat_axis=0, tiled=True)
    length = heads_in.shape[0]
    queries = heads_in[:, 0, 0].reshape(length, heads_loc, HEAD_DIM)
    keys_all = heads_in[:, 1, 0].reshape(length, heads_loc, HEAD_DIM)
    values_all = heads_in[:, 2, 0].reshape(length, heads_loc, HEAD_DIM)
    bias_row = lax.all_gather(key_bias, "seq", axis=1, tiled=True)[0]
    context_heads, log_total = attend_forward(queries, keys_all, values_all, bias_row, score_scale)
    context = lax.all_to_all(
        shortened(context_heads.reshape(length, 1, group_width)),
        "seq",
        split_axis=0,
        concat_axis=1,
        tiled=True,
    ).reshape(tok_rows, model_width)
    attended = hidden_in.astype(jnp.float32) + matmul(context, params[3]) + full_bias_out
    normed = layer_norm(attended, full_gain_attn, full_shift_attn)
    normed_low = normed.astype(jnp.bfloat16)
    pre_act = matmul(normed_low, params[7]) + full_bias_up
    activ = gelu_exact(pre_act).astype(jnp.bfloat16)
    branch_sum = normed + matmul(activ, params[9]) + full_bias_down
    output = layer_norm(branch_sum, full_gain_ffn, full_shift_ffn).astype(jnp.bfloat16)
    matrices = (
        lax.all_gather(w_qkv, "dp", axis=0, tiled=True),
        lax.all_gather(w_out, "dp", axis=0, tiled=True),
        lax.all_gather(w_up, "dp", axis=0, tiled=True),
        lax.all_gather(w_down, "dp", axis=0, tiled=True),
    )
    upstream = grad_out.astype(jnp.float32)
    _, norm_back = jax.vjp(layer_norm, branch_sum, full_gain_ffn, full_shift_ffn)
    d_branch, grad_gain_ffn, grad_shift_ffn = norm_back(upstream)
    grad_bias_down = jnp.sum(d_branch, 0)
    d_branch_low = d_branch.astype(jnp.bfloat16)
    grad_w_down = matmul_left(activ, d_branch_low)
    d_activ = matmul_right(d_branch_low, matrices[3])
    _, gelu_back = jax.vjp(gelu_exact, pre_act)
    d_pre = gelu_back(d_activ)[0]
    grad_bias_up = jnp.sum(d_pre, 0)
    d_pre_low = d_pre.astype(jnp.bfloat16)
    grad_w_up = matmul_left(normed_low, d_pre_low)
    d_normed = d_branch + matmul_right(d_pre_low, matrices[2])
    _, attn_norm_back = jax.vjp(layer_norm, attended, full_gain_attn, full_shift_attn)
    d_attended, grad_gain_attn, grad_shift_attn = attn_norm_back(d_normed)
    grad_bias_out = jnp.sum(d_attended, 0)
    d_attended_low = d_attended.astype(jnp.bfloat16)
    grad_w_out = matmul_left(context, d_attended_low)
    d_context = matmul_right(d_attended_low, matrices[1]).astype(jnp.bfloat16)
    d_context_heads = lax.all_to_all(
        d_context.reshape(tok_rows, groups, group_width),
        "seq",
        split_axis=1,
        concat_axis=0,
        tiled=True,
    )
    query_grad, key_grad, value_grad = attend_backward(
        queries,
        keys_all,
        values_all,
        bias_row,
        score_scale,
        log_total,
        d_context_heads.reshape(length, heads_loc, HEAD_DIM),
    )
    d_heads = (
        jnp.stack([query_grad, key_grad, value_grad], 1)
        .astype(jnp.bfloat16)
        .reshape(length, 3, 1, group_width)
    )
    d_qkv = lax.all_to_all(d_heads, "seq", split_axis=0, concat_axis=2, tiled=True).reshape(
        tok_rows, 3 * model_width
    )
    grad_bias_q = jnp.sum(d_qkv[:, :model_width].astype(jnp.float32), 0)
    grad_bias_v = jnp.sum(d_qkv[:, 2 * model_width :].astype(jnp.float32), 0)
    grad_w_qkv = matmul_left(hidden_in, d_qkv)
    grad_in = d_attended + matmul_right(d_qkv, matrices[0])
    local_grads = (
        grad_w_qkv,
        grad_bias_q,
        grad_bias_v,
        grad_w_out,
        grad_bias_out,
        grad_gain_attn,
        grad_shift_attn,
        grad_w_up,
        grad_bias_up,
        grad_w_down,
        grad_bias_down,
        grad_gain_ffn,
        grad_shift_ffn,
    )
    shares = (
        lax.psum_scatter(
            local_grads[0].astype(jnp.bfloat16), "dp", scatter_dimension=0, tiled=True
        ).astype(jnp.float32),
        lax.psum_scatter(
            local_grads[1].astype(jnp.bfloat16), "dp", scatter_dimension=0, tiled=True
        ).astype(jnp.float32),
        lax.psum_scatter(
            local_grads[2].astype(jnp.bfloat16), "dp", scatter_dimension=0, tiled=True
        ).astype(jnp.float32),
        lax.psum_scatter(
            local_grads[3].astype(jnp.bfloat16), "dp", scatter_dimension=0, tiled=True
        ).astype(jnp.float32),
        lax.psum_scatter(
            local_grads[4].astype(jnp.bfloat16), "dp", scatter_dimension=0, tiled=True
        ).astype(jnp.float32),
        lax.psum_scatter(
            local_grads[5].astype(jnp.bfloat16), "dp", scatter_dimension=0, tiled=True
        ).astype(jnp.float32),
        lax.psum_scatter(
            local_grads[6].astype(jnp.bfloat16), "dp", scatter_dimension=0, tiled=True
        ).astype(jnp.float32),
        lax.psum_scatter(
            local_grads[7].astype(jnp.bfloat16), "dp", scatter_dimension=0, tiled=True
        ).astype(jnp.float32),
        lax.psum_scatter(
            local_grads[8].astype(jnp.bfloat16), "dp", scatter_dimension=0, tiled=True
        ).astype(jnp.float32),
        lax.psum_scatter(
            local_grads[9].astype(jnp.bfloat16), "dp", scatter_dimension=0, tiled=True
        ).astype(jnp.float32),
        lax.psum_scatter(
            local_grads[10].astype(jnp.bfloat16), "dp", scatter_dimension=0, tiled=True
        ).astype(jnp.float32),
        lax.psum_scatter(
            local_grads[11].astype(jnp.bfloat16), "dp", scatter_dimension=0, tiled=True
        ).astype(jnp.float32),
        lax.psum_scatter(
            local_grads[12].astype(jnp.bfloat16), "dp", scatter_dimension=0, tiled=True
        ).astype(jnp.float32),
    )
    owned_grads = (
        lax.psum(shares[0].astype(jnp.bfloat16), "seq").astype(jnp.float32),
        lax.psum(shares[1].astype(jnp.bfloat16), "seq").astype(jnp.float32),
        lax.psum(shares[2].astype(jnp.bfloat16), "seq").astype(jnp.float32),
        lax.psum(shares[3].astype(jnp.bfloat16), "seq").astype(jnp.float32),
        lax.psum(shares[4].astype(jnp.bfloat16), "seq").astype(jnp.float32),
        lax.psum(shares[5].astype(jnp.bfloat16), "seq").astype(jnp.float32),
        lax.psum(shares[6].astype(jnp.bfloat16), "seq").astype(jnp.float32),
        lax.psum(shares[7].astype(jnp.bfloat16), "seq").astype(jnp.float32),
        lax.psum(shares[8].astype(jnp.bfloat16), "seq").astype(jnp.float32),
        lax.psum(shares[9].astype(jnp.bfloat16), "seq").astype(jnp.float32),
        lax.psum(shares[10].astype(jnp.bfloat16), "seq").astype(jnp.float32),
        lax.psum(shares[11].astype(jnp.bfloat16), "seq").astype(jnp.float32),
        lax.psum(shares[12].astype(jnp.bfloat16), "seq").astype(jnp.float32),
    )
    return (
        output,
        grad_in,
        owned_grads[0],
        owned_grads[1],
        owned_grads[2],
        owned_grads[3],
        owned_grads[4],
        owned_grads[5],
        owned_grads[6],
        owned_grads[7],
        owned_grads[8],
        owned_grads[9],
        owned_grads[10],
        owned_grads[11],
        owned_grads[12],
    )


def solution(mesh):
    return jax.shard_map(
        local,
        mesh=mesh,
        in_specs=(
            P(("dp", "seq"), None),
            P("dp", "seq"),
            P("dp", None),
            P("dp"),
            P("dp"),
            P("dp", None),
            P("dp"),
            P("dp"),
            P("dp"),
            P("dp", None),
            P("dp"),
            P("dp", None),
            P("dp"),
            P("dp"),
            P("dp"),
            P(("dp", "seq"), None),
        ),
        out_specs=(
            P(("dp", "seq"), None),
            P(("dp", "seq"), None),
            P("dp", None),
            P("dp"),
            P("dp"),
            P("dp", None),
            P("dp"),
            P("dp"),
            P("dp"),
            P("dp", None),
            P("dp"),
            P("dp", None),
            P("dp"),
            P("dp"),
            P("dp"),
        ),
        check_vma=False,
    )
```

profile of v0, /device:TPU:0, one launch (start us, length us, event | category | flops | bytes accessed | tf_op | source)
XLA Modules:
  0.0 1988.5 jit_solution(5152587531738367793)
XLA Ops:
  9.4 22.5 %all-gather.1 = bf16[8,1,128]{2,1,0:T(2,128)(2,1)S(1)} all-gather(bf16[1,1,128]{2,1,0:T(2,128)(2,1)} %bitcast.231), channel_id=1, replica_groups=mesh['dp'=8,'seq'=4] {'dp'}, dimensions={0}, use_global_device_ids=true | all-gather | bytes 2304 | tf_op jit(solution)/shard_map/all_gather | solution.py:172
  48.6 63.4 %all-gather.14.cloned.1.call-done = bf16[1024,3072]{1,0:T(8,128)(2,1)} async-done(((bf16[128,3072]{1,0:T(8,128)(2,1)}), bf16[1024,3072]{1,0:T(8,128)(2,1)}) %all-gather.14.cloned.1.call-update) | async-done | bytes 6291472 | tf_op jit(solution)/shard_map/all_gather | solution.py:170
  141.7 54.1 %all_gather.49 = f32[1,3072]{1,0:T(1,128)S(1)} all-gather(f32[1,768]{1,0:T(1,128)S(1)} %copy-done.34), channel_id=1, replica_groups=mesh['dp'=8,'seq'=4] {'seq'}, dimensions={1}, use_global_device_ids=true | all-gather | bytes 15360 | tf_op jit(solution)/shard_map/all_gather | solution.py:205
  213.4 180.6 %while.27 = (s32[]{:T(128)}, bf16[6,512,4,64]{1,3,2,0:T(8,128)(2,1)}, f32[6,4,512]{2,1,0:T(4,128)S(1)}, bf16[6,512,4,64]{1,3,2,0:T(8,128)(2,1)}, bf16[3072,4,64]...) while((s32[]{:T(128)}, bf16[6,512,4,64]{1,3,2,0:T(8,128)(2,1)}, ...), condition=%wide.region_5.6_spmd, body=%wide.region_0.5_spmd.sunk | while | flops 1686765568 | bytes 80098904 | solution.py:81
  399.7 22.8 %reshape.246 = bf16[3072,1,256]{2,1,0:T(2,128)(2,1)} reshape(bf16[6,512,4,64]{3,2,1,0:T(4,128)(2,1)} %copy.114) | data formatting | bytes 3145728 | tf_op jit(solution)/shard_map/reshape;reshape | solution.py:208
  445.9 17.5 all-gather.2
  480.2 17.5 all-gather.4
  497.7 26.0 %all-gather.5 = bf16[8,1,512]{2,1,0:T(2,128)(2,1)S(1)} all-gather(bf16[1,1,512]{2,1,0:T(2,128)(2,1)S(1)} %reshape.229), channel_id=1, replica_groups=mesh['dp'=8,'seq'=4] {'dp'}, dimensions={0}, use_global_device_ids=true | all-gather | bytes 9216 | tf_op jit(solution)/shard_map/all_gather | solution.py:178
  539.9 18.2 all-gather.7
  586.4 39.4 %multiply_convert_fusion.2 = (bf16[768,4096]{1,0:T(8,128)(2,1)}, f32[768,4096]{1,0:T(8,128)}, f32[768,4096]{1,0:T(8,128)}) fusion(f32[4096]{0:T(1024)S(1)} %bitcast.222, bf16[1024,4096]{1,0:T(8,128)(2,1)} %all-gather.18.cloned.1.call-done, f32[768,1024]{1,0:T(8,128)S(1)} %get-tuple-element.410, f32[1024]{0:T(1024)S(1)} %bitcast.226, ...), kind=kOutput, calls=%fused_computation.100 | convolution fusion | flops 6654001152 | bytes 43022336 | tf_op jit(solution)/shard_map/dot_general | solution.py:30
  642.8 21.7 %fusion.106 = (bf16[4096]{0:T(1024)(128)(2,1)}, bf16[768,4096]{1,0:T(8,128)(2,1)}) fusion(f32[768,4096]{1,0:T(8,128)} %get-tuple-element.392, bf16[4096,1024]{1,0:T(8,128)(2,1)} %all-gather.20.cloned.1.call-done, f32[768,1024]{1,0:T(8,128)} %get-tuple-element.390, f32[768]{0:T(1024)S(1)} %negate_multiply_fusion.2, f32[768,4096]{1,0:T(8,128)} %get-tuple-element.411, ...), kind=kOutput, calls=%fused_computation.167 | convolution fusion | flops 6494351360 | bytes 43019264 | tf_op jit(solution)/shard_map/dot_general | solution.py:40
  687.8 20.0 %all-to-all-done.2 = bf16[768,4,256]{0,2,1:T(8,128)(2,1)S(1)} async-done(((bf16[768,4,256]{0,2,1:T(8,128)(2,1)}), bf16[768,4,256]{0,2,1:T(8,128)(2,1)S(1)}, u32[]{:S(2)}, u32[]{:S(2)}) %all-to-all-start.2) | async-done | bytes 1572896 | tf_op jit(solution)/shard_map/all_to_all | solution.py:246
  717.6 568.6 %while.28 = (s32[]{:T(128)}, f32[3072,4,64]{0,2,1:T(8,128)}, f32[3072,4,64]{0,2,1:T(8,128)}, bf16[6,512,4,64]{1,3,2,0:T(8,128)(2,1)}, bf16[6,512,4,64]{1,3,2,0:T...) while((s32[]{:T(128)}, f32[3072,4,64]{0,2,1:T(8,128)}, ...), condition=%wide.region_17.18_spmd.clone, body=%wide.region_14.17_spmd.clone.sunk | while | flops 4127193088 | bytes 341160832 | solution.py:144
  740.8 20.1 %multiply_reduce_fusion.7 = (f32[2,512]{1,0:T(2,128)S(1)}, f32[2,512]{1,0:T(2,128)S(1)}, f32[2,512,3072]{2,1,0:T(8,128)}) fusion(f32[2,512,3072]{2,1,0:T(8,128)} %fusion.191, f32[2,512]{1,0:T(2,128)S(1)} %get-tuple-element.546, f32[3072]{0:T(1024)S(1)} %bitcast.204, f32[2,512,3072]{2,1,0:T(8,128)} %fusion.192, f32[2,512]{1,0:T(2,128)S(1)} %get-tuple-element.547, ...), kind=kOutput, calls=%fused_computation.39.clone.1 | convolution fusion | flops 434108416 | bytes 51409408 | tf_op jit(solution)/shard_map/while/body/eval_jaxpr/bhe,lhe->hbl/dot_general | solution.py:111
  760.9 17.9 multiply_convert_fusion.4
  834.0 20.1 %multiply_reduce_fusion.7 = (f32[2,512]{1,0:T(2,128)S(1)}, f32[2,512]{1,0:T(2,128)S(1)}, f32[2,512,3072]{2,1,0:T(8,128)}) fusion(f32[2,512,3072]{2,1,0:T(8,128)} %fusion.191, f32[2,512]{1,0:T(2,128)S(1)} %get-tuple-element.546, f32[3072]{0:T(1024)S(1)} %bitcast.204, f32[2,512,3072]{2,1,0:T(8,128)} %fusion.192, f32[2,512]{1,0:T(2,128)S(1)} %get-tuple-element.547, ...), kind=kOutput, calls=%fused_computation.39.clone.1 | convolution fusion | flops 434108416 | bytes 51409408 | tf_op jit(solution)/shard_map/while/body/eval_jaxpr/bhe,lhe->hbl/dot_general | solution.py:111
  854.0 17.9 multiply_convert_fusion.4
  928.9 20.0 %multiply_reduce_fusion.7 = (f32[2,512]{1,0:T(2,128)S(1)}, f32[2,512]{1,0:T(2,128)S(1)}, f32[2,512,3072]{2,1,0:T(8,128)}) fusion(f32[2,512,3072]{2,1,0:T(8,128)} %fusion.191, f32[2,512]{1,0:T(2,128)S(1)} %get-tuple-element.546, f32[3072]{0:T(1024)S(1)} %bitcast.204, f32[2,512,3072]{2,1,0:T(8,128)} %fusion.192, f32[2,512]{1,0:T(2,128)S(1)} %get-tuple-element.547, ...), kind=kOutput, calls=%fused_computation.39.clone.1 | convolution fusion | flops 434108416 | bytes 51409408 | tf_op jit(solution)/shard_map/while/body/eval_jaxpr/bhe,lhe->hbl/dot_general | solution.py:111
  948.9 17.9 multiply_convert_fusion.4
  1023.8 20.1 %multiply_reduce_fusion.7 = (f32[2,512]{1,0:T(2,128)S(1)}, f32[2,512]{1,0:T(2,128)S(1)}, f32[2,512,3072]{2,1,0:T(8,128)}) fusion(f32[2,512,3072]{2,1,0:T(8,128)} %fusion.191, f32[2,512]{1,0:T(2,128)S(1)} %get-tuple-element.546, f32[3072]{0:T(1024)S(1)} %bitcast.204, f32[2,512,3072]{2,1,0:T(8,128)} %fusion.192, f32[2,512]{1,0:T(2,128)S(1)} %get-tuple-element.547, ...), kind=kOutput, calls=%fused_computation.39.clone.1 | convolution fusion | flops 434108416 | bytes 51409408 | tf_op jit(solution)/shard_map/while/body/eval_jaxpr/bhe,lhe->hbl/dot_general | solution.py:111
  1043.9 17.9 multiply_convert_fusion.4
  1118.9 20.0 %multiply_reduce_fusion.7 = (f32[2,512]{1,0:T(2,128)S(1)}, f32[2,512]{1,0:T(2,128)S(1)}, f32[2,512,3072]{2,1,0:T(8,128)}) fusion(f32[2,512,3072]{2,1,0:T(8,128)} %fusion.191, f32[2,512]{1,0:T(2,128)S(1)} %get-tuple-element.546, f32[3072]{0:T(1024)S(1)} %bitcast.204, f32[2,512,3072]{2,1,0:T(8,128)} %fusion.192, f32[2,512]{1,0:T(2,128)S(1)} %get-tuple-element.547, ...), kind=kOutput, calls=%fused_computation.39.clone.1 | convolution fusion | flops 434108416 | bytes 51409408 | tf_op jit(solution)/shard_map/while/body/eval_jaxpr/bhe,lhe->hbl/dot_general | solution.py:111
  1138.9 17.9 multiply_convert_fusion.4
  1213.8 20.1 %multiply_reduce_fusion.7 = (f32[2,512]{1,0:T(2,128)S(1)}, f32[2,512]{1,0:T(2,128)S(1)}, f32[2,512,3072]{2,1,0:T(8,128)}) fusion(f32[2,512,3072]{2,1,0:T(8,128)} %fusion.191, f32[2,512]{1,0:T(2,128)S(1)} %get-tuple-element.546, f32[3072]{0:T(1024)S(1)} %bitcast.204, f32[2,512,3072]{2,1,0:T(8,128)} %fusion.192, f32[2,512]{1,0:T(2,128)S(1)} %get-tuple-element.547, ...), kind=kOutput, calls=%fused_computation.39.clone.1 | convolution fusion | flops 434108416 | bytes 51409408 | tf_op jit(solution)/shard_map/while/body/eval_jaxpr/bhe,lhe->hbl/dot_general | solution.py:111
  1233.9 17.9 multiply_convert_fusion.4
  1309.3 74.6 %all_to_all.63 = bf16[3072,3,1,256]{3,1,2,0:T(4,128)(2,1)S(1)} all-to-all(bf16[3072,3,1,256]{3,1,2,0:T(4,128)(2,1)} %copy.110), channel_id=1, replica_groups=mesh['dp'=8,'seq'=4] {'seq'}, dimensions={0} | all-to-all | bytes 9437184 | tf_op jit(solution)/shard_map/all_to_all | solution.py:267
  1453.9 36.6 %all-reduce.9 = (bf16[1024]{0:T(1024)(128)(2,1)S(1)}, bf16[1024]{0:T(1024)(128)(2,1)S(1)}, bf16[1024]{0:T(1024)(128)(2,1)S(1)}, bf16[1024]{0:T(1024)(128)(2,1)S(...) all-reduce(bf16[1024]{0:T(1024)(128)(2,1)S(1)} %get-tuple-element.3, ...), channel_id=3, replica_groups=mesh['dp'=8,'seq'=4] {'dp'}, use_global_device_ids=true, to_apply=%region_21.22.clone | all-reduce | flops 12288 | bytes 49152
  1501.6 26.6 %reduce-scatter.13.cloned.1.call-done = bf16[128,3072]{1,0:T(8,128)(2,1)} async-done(((bf16[1024,3072]{1,0:T(8,128)(2,1)}), bf16[128,3072]{1,0:T(8,128)(2,1)}) %reduce-scatter.13.cloned.1.call-update) | async-done | bytes 786448
  1530.4 68.5 %reduce-scatter.7.cloned.1.call-done = bf16[128,1024]{1,0:T(8,128)(2,1)} async-done(((bf16[1024,1024]{1,0:T(8,128)(2,1)}), bf16[128,1024]{1,0:T(8,128)(2,1)}) %reduce-scatter.7.cloned.1.call-update) | async-done | bytes 262160 | tf_op jit(solution)/shard_map/reduce_scatter | solution.py:299
  1598.9 151.6 %reduce-scatter.11.cloned.1.call-done = bf16[512,1024]{1,0:T(8,128)(2,1)} async-done(((bf16[4096,1024]{1,0:T(8,128)(2,1)}), bf16[512,1024]{1,0:T(8,128)(2,1)}) %reduce-scatter.11.cloned.1.call-update) | async-done | bytes 1048592 | tf_op jit(solution)/shard_map/reduce_scatter | solution.py:317
  1750.6 152.1 %reduce-scatter.9.cloned.1.call-done = bf16[128,4096]{1,0:T(8,128)(2,1)} async-done(((bf16[1024,4096]{1,0:T(8,128)(2,1)}), bf16[128,4096]{1,0:T(8,128)(2,1)}) %reduce-scatter.9.cloned.1.call-update) | async-done | bytes 1048592 | tf_op jit(solution)/shard_map/reduce_scatter | solution.py:311
  1912.6 61.3 %all-reduce.14.cloned.1.call-done = (bf16[128,3072]{0,1:T(8,128)(2,1)}, bf16[128,1024]{1,0:T(8,128)(2,1)}, bf16[128,4096]{1,0:T(8,128)(2,1)}, bf16[512,1024]{1,0:T(8,128)(2,1)}) async-done(((bf16[128,3072]{0,1:T(8,128)(2,1)}, bf16[128,1024]{1,0:T(8,128)(2,1)}, bf16[128,4096]{1,0:T(8,128)(2,1)}, bf16[512,1024]{1,0:T(8,128)(2,1)}), (bf16[128,3072]{0,1:T(8,128)(2,1)}, bf16[128,1024]{1,0:T(8,128)(2,1)}, ...) | async-done | bytes 3145744 | tf_op jit(solution)/shard_map/psum | solution.py:331
  (445 shorter events, 848.9 us)
Async XLA Ops:
  7.2 104.8 %all-gather.14.cloned.1.call-start = ((), (), s32[]{:S(2)}) async-start(), calls=%async_computation.8 | async-start | bytes 7077888 | tf_op jit(solution)/shard_map/all_gather | solution.py:170
  7.9 573.4 %all-gather.16.cloned.1.call-start = ((), (), s32[]{:S(2)}) async-start(), calls=%async_computation.9 | async-start | bytes 2359296 | tf_op jit(solution)/shard_map/all_gather | solution.py:173
  8.7 577.7 %all-gather.18.cloned.1.call-start = ((), (), s32[]{:S(2)}) async-start(), calls=%async_computation.10 | async-start | bytes 9437184 | tf_op jit(solution)/shard_map/all_gather | solution.py:177
  135.9 59.9 %all-to-all-start = ((bf16[768,3,4,256]{3,0,1,2:T(8,128)(2,1)}), bf16[768,3,4,256]{3,0,1,2:T(8,128)(2,1)}, u32[]{:S(2)}, u32[]{:S(2)}) async-start(bf16[768,3,4,256]{3,0,1,2:T(8,128)(2,1)} %copy.96), calls=%async_computation | async-start | bytes 9437184 | tf_op jit(solution)/shard_map/all_to_all | solution.py:200
  141.1 484.7 %all-gather.20.cloned.1.call-start = ((), (), s32[]{:S(2)}) async-start(), calls=%async_computation.11 | async-start | bytes 9437184 | tf_op jit(solution)/shard_map/all_gather | solution.py:179
  394.0 28.4 %copy-start.1 = (bf16[3072,4,64]{0,2,1:T(8,128)(2,1)}, bf16[3072,4,64]{0,2,1:T(8,128)(2,1)S(1)}, u32[]{:S(2)}) copy-start(bf16[3072,4,64]{0,2,1:T(8,128)(2,1)S(1)} %get-tuple-element.634) | copy-start | bytes 4718596
  394.0 28.4 %copy-start.14 = (f32[1,3072]{1,0:T(1,128)}, f32[1,3072]{1,0:T(1,128)S(1)}, u32[]{:S(2)}) copy-start(f32[1,3072]{1,0:T(1,128)S(1)} %get-tuple-element.653) | copy-start | bytes 36868
  394.0 28.4 %copy-start.21 = (f32[6,4,512]{2,1,0:T(4,128)}, f32[6,4,512]{2,1,0:T(4,128)S(1)}, u32[]{:S(2)}) copy-start(f32[6,4,512]{2,1,0:T(4,128)S(1)} %get-tuple-element.586) | copy-start | bytes 147460
  422.9 22.9 %copy-start.38 = (bf16[128]{0:T(256)(128)(2,1)S(1)}, bf16[128]{0:T(256)(128)(2,1)}, u32[]{:S(2)}) copy-start(bf16[128]{0:T(256)(128)(2,1)} %param.26) | copy-start | bytes 772
  422.9 40.4 %copy-start.39 = (bf16[128]{0:T(256)(128)(2,1)S(1)}, bf16[128]{0:T(256)(128)(2,1)}, u32[]{:S(2)}) copy-start(bf16[128]{0:T(256)(128)(2,1)} %param.27) | copy-start | bytes 772
  422.9 57.3 %copy-start.40 = (bf16[128]{0:T(256)(128)(2,1)S(1)}, bf16[128]{0:T(256)(128)(2,1)}, u32[]{:S(2)}) copy-start(bf16[128]{0:T(256)(128)(2,1)} %param.28) | copy-start | bytes 772
  422.9 74.8 %copy-start.37 = (bf16[512]{0:T(512)(128)(2,1)S(1)}, bf16[512]{0:T(512)(128)(2,1)}, u32[]{:S(2)}) copy-start(bf16[512]{0:T(512)(128)(2,1)} %param.30) | copy-start | bytes 3076
  422.9 100.8 %copy-start.41 = (bf16[128]{0:T(256)(128)(2,1)S(1)}, bf16[128]{0:T(256)(128)(2,1)}, u32[]{:S(2)}) copy-start(bf16[128]{0:T(256)(128)(2,1)} %param.32) | copy-start | bytes 772
  423.0 117.0 %copy-start.42 = (bf16[128]{0:T(256)(128)(2,1)S(1)}, bf16[128]{0:T(256)(128)(2,1)}, u32[]{:S(2)}) copy-start(bf16[128]{0:T(256)(128)(2,1)} %param.33) | copy-start | bytes 772
  423.0 135.1 %copy-start.43 = (bf16[128]{0:T(256)(128)(2,1)S(1)}, bf16[128]{0:T(256)(128)(2,1)}, u32[]{:S(2)}) copy-start(bf16[128]{0:T(256)(128)(2,1)} %param.34) | copy-start | bytes 772
  441.5 132.8 %all-to-all-start.1 = ((bf16[4,2,98304]{2,1,0:T(2,128)(2,1)}), bf16[4,2,98304]{2,1,0:T(2,128)(2,1)}, u32[]{:S(2)}, u32[]{:S(2)}) async-start(bf16[4,2,98304]{2,1,0:T(2,128)(2,1)} %reshape.259), calls=%async_computation.1 | async-start | bytes 3145728 | tf_op jit(solution)/shard_map/all_to_all | solution.py:207
  480.2 197.7 %copy-start.24 = (f32[8,1,128]{2,1,0:T(1,128)}, f32[8,1,128]{2,1,0:T(1,128)S(1)}, u32[]{:S(2)}) copy-start(f32[8,1,128]{2,1,0:T(1,128)S(1)} %convert_element_type.240) | copy-start | bytes 12292
  497.7 128.1 %copy-start.32 = (f32[8,1,128]{2,1,0:T(1,128)}, f32[8,1,128]{2,1,0:T(1,128)S(1)}, u32[]{:S(2)}) copy-start(f32[8,1,128]{2,1,0:T(1,128)S(1)} %convert_element_type.241) | copy-start | bytes 12292
  585.9 92.1 %copy-start.8 = (f32[768,1024]{1,0:T(8,128)}, f32[768,1024]{1,0:T(8,128)S(1)}, u32[]{:S(2)}) copy-start(f32[768,1024]{1,0:T(8,128)S(1)} %get-tuple-element.410) | copy-start | bytes 9437188
  585.9 92.1 %copy-start.19 = (f32[768]{0:T(1024)}, f32[768]{0:T(1024)S(1)}, u32[]{:S(2)}) copy-start(f32[768]{0:T(1024)S(1)} %broadcast_multiply_fusion.1) | copy-start | bytes 9220
  586.4 91.6 %copy-start.26 = (f32[768]{0:T(1024)}, f32[768]{0:T(1024)S(1)}, u32[]{:S(2)}) copy-start(f32[768]{0:T(1024)S(1)} %fusion.94) | copy-start | bytes 9220
  642.8 21.7 %copy-start.28 = (f32[768]{0:T(1024)}, f32[768]{0:T(1024)S(1)}, u32[]{:S(2)}) copy-start(f32[768]{0:T(1024)S(1)} %negate_multiply_fusion.2) | copy-start | bytes 9220
  684.1 23.6 %all-to-all-start.2 = ((bf16[768,4,256]{0,2,1:T(8,128)(2,1)}), bf16[768,4,256]{0,2,1:T(8,128)(2,1)S(1)}, u32[]{:S(2)}, u32[]{:S(2)}) async-start(bf16[768,4,256]{0,2,1:T(8,128)(2,1)} %bitcast.33), calls=%async_computation.2 | async-start | bytes 3145728 | tf_op jit(solution)/shard_map/all_to_all | solution.py:246
  687.7 840.5 %reduce-scatter.13.cloned.1.call-start = ((), (), s32[]{:S(2)}) async-start(), calls=%async_computation.15 | async-start | bytes 7077888
  871.9 15.6 slice-start.3
  966.8 15.6 slice-start.3
  1061.8 15.6 slice-start.3
  1411.6 187.3 %reduce-scatter.7.cloned.1.call-start = ((), (), s32[]{:S(2)}) async-start(), calls=%async_computation.12 | async-start | bytes 2359296 | tf_op jit(solution)/shard_map/reduce_scatter | solution.py:299
  1418.0 332.5 %reduce-scatter.11.cloned.1.call-start = ((), (), s32[]{:S(2)}) async-start(), calls=%async_computation.14 | async-start | bytes 9437184 | tf_op jit(solution)/shard_map/reduce_scatter | solution.py:317
  1430.6 472.1 %reduce-scatter.9.cloned.1.call-start = ((), (), s32[]{:S(2)}) async-start(), calls=%async_computation.13 | async-start | bytes 9437184 | tf_op jit(solution)/shard_map/reduce_scatter | solution.py:311
  1444.9 529.0 %all-reduce.14.cloned.1.call-start = ((), (), s32[]{:S(2)}) async-start(), calls=%async_computation.16 | async-start | bytes 6291456 | tf_op jit(solution)/shard_map/psum | solution.py:331
  1451.3 451.4 %copy-start.12 = (f32[768,1024]{1,0:T(8,128)S(1)}, f32[768,1024]{1,0:T(8,128)}, u32[]{:S(2)}) copy-start(f32[768,1024]{1,0:T(8,128)} %copy-done.10) | copy-start | bytes 9437188
  (73 other events, 488.5 us)
Sparse Core Ops, SparseCore 0:
  10.2 101.7 all-gather.13
  114.1 47.4 all-gather.15
  163.8 123.4 all-gather.17
  289.2 123.1 all-gather.19
  1411.7 116.4 reduce-scatter.12
  1532.1 66.7 reduce-scatter.6
  1602.5 147.9 reduce-scatter.10
  1754.6 148.0 reduce-scatter.8
  1905.9 67.9 all-reduce.13
where the time goes:
time: 2000 us; the launch traced here: 1990 us
  matrix products  711 us (36%)
  waiting for transfers between devices  546 us (27%)
  blocking collectives  339 us (17%)
  other arithmetic  225 us (11%)
  local copies, waits for them, and re-layouts  137 us (7%)
    dot_general x24, matrix products, one_block(): jnp.einsum('bhe,lhe->hbl', query_blk[:, part], keys_all[:, part], preferr...  181 us
    dot_general x12, matrix products, one_block(): jnp.einsum('bhe,lhe->hbl', grad_blk[:, part], values_all[:, part], prefer...  167 us
    reduce_scatter x1, waiting for transfers between devices, local(): lax.psum_scatter(local_grads[7].astype(jnp.bfloat16), 'dp', scatter_dimen...  152 us
    reduce_scatter x1, waiting for transfers between devices, local(): lax.psum_scatter(local_grads[9].astype(jnp.bfloat16), 'dp', scatter_dimen...  152 us
    convert_element_type x6, other arithmetic, one_block(): d_scores = (probs_full * (d_probs - row_dot)).astype(jnp.bfloat16)  107 us
    all_to_all x1, blocking collectives, local(): lax.all_to_all(d_heads, 'seq', split_axis=0, concat_axis=2, tiled=True)  74.6 us
    reduce_scatter x1, waiting for transfers between devices, local(): lax.psum_scatter(local_grads[3].astype(jnp.bfloat16), 'dp', scatter_dimen...  68.5 us
    dot_general x12, matrix products, one_block(): jnp.einsum('hbl,lhe->bhe', probs_low, values_all[:, part], preferred_elem...  66.6 us
  transfers between devices with their start and end apart: 12, of which 7 were waited for; matrix products, arithmetic and copies ran while one was open for 19% of the time, Pallas kernels for 0%

commit v1 on v0

--- a/solution.py
+++ b/solution.py
@@ -328,7 +328,7 @@
         ).astype(jnp.float32),
     )
     owned_grads = (
-        lax.psum(shares[0].astype(jnp.bfloat16), "seq").astype(jnp.float32),
+        jnp.sum(lax.all_gather(shares[0].astype(jnp.bfloat16), "seq"), axis=0).astype(jnp.float32),
         lax.psum(shares[1].astype(jnp.bfloat16), "seq").astype(jnp.float32),
         lax.psum(shares[2].astype(jnp.bfloat16), "seq").astype(jnp.float32),
         lax.psum(shares[3].astype(jnp.bfloat16), "seq").astype(jnp.float32),

time: 2000 us -> 1680 us (0.84)
  waiting for transfers between devices: 546 us -> 205 us
  other arithmetic: 225 us -> 245 us
    reduce_scatter x1, waiting for transfers between devices: 152 us -> 0.02 us  [local(): lax.psum_scatter(local_grads[7].astype(jnp.bfloat16), 'dp', scatter_dimen...]
    reduce_scatter x1, waiting for transfers between devices: 152 us -> 0.02 us  [local(): lax.psum_scatter(local_grads[9].astype(jnp.bfloat16), 'dp', scatter_dimen...]
    unnamed x10 -> x11, waiting for transfers between devices: 29.3 us -> 119 us
    reduce_scatter x1, waiting for transfers between devices: 68.5 us -> 0.02 us  [local(): lax.psum_scatter(local_grads[3].astype(jnp.bfloat16), 'dp', scatter_dimen...]
    psum x1, waiting for transfers between devices: 61.3 us -> 0.01 us  [local(): lax.psum(shares[3].astype(jnp.bfloat16), 'seq').astype(jnp.float32)]
  transfers between devices with their start and end apart: 12 -> 13, of which waited for: 7 -> 4; matrix products, arithmetic and copies ran while one was open for 19% -> 61% of each run, Pallas kernels for 0% -> 0%
where the time goes in v1:
time: 1680 us; the launch traced here: 1670 us
  matrix products  715 us (43%)
  blocking collectives  338 us (20%)
  other arithmetic  245 us (15%)
  waiting for transfers between devices  205 us (12%)
  local copies, waits for them, and re-layouts  136 us (8%)
    dot_general x24, matrix products, one_block(): jnp.einsum('bhe,lhe->hbl', query_blk[:, part], keys_all[:, part], preferr...  181 us
    dot_general x12, matrix products, one_block(): jnp.einsum('bhe,lhe->hbl', grad_blk[:, part], values_all[:, part], prefer...  169 us
    unnamed x11, waiting for transfers between devices  119 us
    convert_element_type x6, other arithmetic, one_block(): d_scores = (probs_full * (d_probs - row_dot)).astype(jnp.bfloat16)  109 us
    all_to_all x1, blocking collectives, local(): lax.all_to_all(d_heads, 'seq', split_axis=0, concat_axis=2, tiled=True)  74.6 us
    dot_general x12, matrix products, one_block(): jnp.einsum('hbl,lhe->bhe', probs_low, values_all[:, part], preferred_elem...  66.6 us
    dot_general x4, matrix products, matmul(): return jnp.dot(left, right, preferred_element_type=jnp.float32)  64.2 us
    all_gather x1, waiting for transfers between devices, local(): lax.all_gather(w_qkv, 'dp', axis=0, tiled=True)  63.4 us
  transfers between devices with their start and end apart: 13, of which 4 were waited for; matrix products, arithmetic and copies ran while one was open for 61% of the time, Pallas kernels for 0%

profile of v1, /device:TPU:0, one launch (start us, length us, event | category | flops | bytes accessed | tf_op | source)
XLA Modules:
  0.0 1670.7 jit_solution(2083846623087121450)
XLA Ops:
  9.4 22.5 %all-gather.2 = bf16[8,1,128]{2,1,0:T(2,128)(2,1)S(1)} all-gather(bf16[1,1,128]{2,1,0:T(2,128)(2,1)} %bitcast.233), channel_id=1, replica_groups=mesh['dp'=8,'seq'=4] {'dp'}, dimensions={0}, use_global_device_ids=true | all-gather | bytes 2304 | tf_op jit(solution)/shard_map/all_gather | solution.py:172
  31.9 16.7 %all-gather.1 = bf16[8,1,128]{2,1,0:T(2,128)(2,1)S(1)} all-gather(bf16[1,1,128]{2,1,0:T(2,128)(2,1)} %bitcast.234), channel_id=1, replica_groups=mesh['dp'=8,'seq'=4] {'dp'}, dimensions={0}, use_global_device_ids=true | all-gather | bytes 2304 | tf_op jit(solution)/shard_map/all_gather | solution.py:171
  48.6 63.4 %all-gather.16.cloned.1.call-done = bf16[1024,3072]{1,0:T(8,128)(2,1)} async-done(((bf16[128,3072]{1,0:T(8,128)(2,1)}), bf16[1024,3072]{1,0:T(8,128)(2,1)}) %all-gather.16.cloned.1.call-update) | async-done | bytes 6291472 | tf_op jit(solution)/shard_map/all_gather | solution.py:170
  141.8 54.1 %all_gather.55 = f32[1,3072]{1,0:T(1,128)S(1)} all-gather(f32[1,768]{1,0:T(1,128)S(1)} %copy-done.22), channel_id=1, replica_groups=mesh['dp'=8,'seq'=4] {'seq'}, dimensions={1}, use_global_device_ids=true | all-gather | bytes 15360 | tf_op jit(solution)/shard_map/all_gather | solution.py:205
  213.5 180.5 %while.27 = (s32[]{:T(128)}, bf16[6,512,4,64]{1,3,2,0:T(8,128)(2,1)}, f32[6,4,512]{2,1,0:T(4,128)S(1)}, bf16[6,512,4,64]{1,3,2,0:T(8,128)(2,1)}, bf16[3072,4,64]...) while((s32[]{:T(128)}, bf16[6,512,4,64]{1,3,2,0:T(8,128)(2,1)}, ...), condition=%wide.region_5.6_spmd, body=%wide.region_0.5_spmd.sunk | while | flops 1686765568 | bytes 80098904 | solution.py:81
  399.7 22.8 %reshape.247 = bf16[3072,1,256]{2,1,0:T(2,128)(2,1)} reshape(bf16[6,512,4,64]{3,2,1,0:T(4,128)(2,1)} %copy.111) | data formatting | bytes 3145728 | tf_op jit(solution)/shard_map/reshape;reshape | solution.py:208
  423.0 16.7 reduce.4
  446.0 17.4 %all-gather.3 = bf16[8,1,128]{2,1,0:T(2,128)(2,1)S(1)} all-gather(bf16[1,1,128]{2,1,0:T(2,128)(2,1)S(1)} %bitcast.235), channel_id=1, replica_groups=mesh['dp'=8,'seq'=4] {'dp'}, dimensions={0}, use_global_device_ids=true | all-gather | bytes 2304 | tf_op jit(solution)/shard_map/all_gather | solution.py:174
  463.4 17.0 %all-gather.4 = bf16[8,1,128]{2,1,0:T(2,128)(2,1)S(1)} all-gather(bf16[1,1,128]{2,1,0:T(2,128)(2,1)S(1)} %bitcast.236), channel_id=1, replica_groups=mesh['dp'=8,'seq'=4] {'dp'}, dimensions={0}, use_global_device_ids=true | all-gather | bytes 2304 | tf_op jit(solution)/shard_map/all_gather | solution.py:175
  480.4 17.4 %all-gather.5 = bf16[8,1,128]{2,1,0:T(2,128)(2,1)S(1)} all-gather(bf16[1,1,128]{2,1,0:T(2,128)(2,1)S(1)} %bitcast.237), channel_id=1, replica_groups=mesh['dp'=8,'seq'=4] {'dp'}, dimensions={0}, use_global_device_ids=true | all-gather | bytes 2304 | tf_op jit(solution)/shard_map/all_gather | solution.py:176
  497.8 26.0 %all-gather.6 = bf16[8,1,512]{2,1,0:T(2,128)(2,1)S(1)} all-gather(bf16[1,1,512]{2,1,0:T(2,128)(2,1)S(1)} %reshape.230), channel_id=1, replica_groups=mesh['dp'=8,'seq'=4] {'dp'}, dimensions={0}, use_global_device_ids=true | all-gather | bytes 9216 | tf_op jit(solution)/shard_map/all_gather | solution.py:178
  523.8 16.2 all-gather.7
  540.0 18.2 %all-gather.8 = bf16[8,1,128]{2,1,0:T(2,128)(2,1)S(1)} all-gather(bf16[1,1,128]{2,1,0:T(2,128)(2,1)S(1)} %bitcast.239), channel_id=1, replica_groups=mesh['dp'=8,'seq'=4] {'dp'}, dimensions={0}, use_global_device_ids=true | all-gather | bytes 2304 | tf_op jit(solution)/shard_map/all_gather | solution.py:181
  586.4 38.7 %multiply_convert_fusion.2 = (bf16[768,4096]{1,0:T(8,128)(2,1)}, f32[768,4096]{1,0:T(8,128)}, f32[768,4096]{1,0:T(8,128)}) fusion(f32[4096]{0:T(1024)S(1)} %bitcast.224, bf16[1024,4096]{1,0:T(8,128)(2,1)} %all-gather.20.cloned.1.call-done, f32[768,1024]{1,0:T(8,128)S(1)} %get-tuple-element.364, f32[1024]{0:T(1024)S(1)} %bitcast.228, ...), kind=kOutput, calls=%fused_computation.100 | convolution fusion | flops 6654001152 | bytes 43022336 | tf_op jit(solution)/shard_map/dot_general | solution.py:30
  642.3 21.6 %fusion.106 = (bf16[4096]{0:T(1024)(128)(2,1)}, bf16[768,4096]{1,0:T(8,128)(2,1)}) fusion(f32[768,4096]{1,0:T(8,128)} %get-tuple-element.346, bf16[4096,1024]{1,0:T(8,128)(2,1)} %all-gather.22.cloned.1.call-done, f32[768,1024]{1,0:T(8,128)} %get-tuple-element.344, f32[768]{0:T(1024)S(1)} %negate_multiply_fusion.2, f32[768,4096]{1,0:T(8,128)} %get-tuple-element.365, ...), kind=kOutput, calls=%fused_computation.167 | convolution fusion | flops 6494351360 | bytes 43019264 | tf_op jit(solution)/shard_map/dot_general | solution.py:40
  736.2 573.3 %while.28 = (s32[]{:T(128)}, f32[3072,4,64]{0,2,1:T(8,128)}, f32[3072,4,64]{0,2,1:T(8,128)}, bf16[6,512,4,64]{1,3,2,0:T(8,128)(2,1)}, bf16[6,512,4,64]{1,3,2,0:T...) while((s32[]{:T(128)}, f32[3072,4,64]{0,2,1:T(8,128)}, ...), condition=%wide.region_17.18_spmd.clone, body=%wide.region_14.17_spmd.clone.sunk | while | flops 4127193088 | bytes 341160832 | solution.py:144
  759.3 20.9 %multiply_reduce_fusion.7 = (f32[2,512]{1,0:T(2,128)S(1)}, f32[2,512]{1,0:T(2,128)S(1)}, f32[2,512,3072]{2,1,0:T(8,128)}) fusion(f32[2,512,3072]{2,1,0:T(8,128)} %fusion.191, f32[2,512]{1,0:T(2,128)S(1)} %get-tuple-element.500, f32[3072]{0:T(1024)S(1)} %bitcast.206, f32[2,512,3072]{2,1,0:T(8,128)} %fusion.192, f32[2,512]{1,0:T(2,128)S(1)} %get-tuple-element.501, ...), kind=kOutput, calls=%fused_computation.39.clone.1 | convolution fusion | flops 434108416 | bytes 51409408 | tf_op jit(solution)/shard_map/while/body/eval_jaxpr/bhe,lhe->hbl/dot_general | solution.py:111
  780.2 18.8 %multiply_convert_fusion.4 = (bf16[2,512,3072]{2,1,0:T(8,128)(2,1)S(1)}, bf16[2,512,3072]{2,1,0:T(8,128)(2,1)S(1)}) fusion(f32[2,512,3072]{2,1,0:T(8,128)} %get-tuple-element.502, f32[2,512,3072]{2,1,0:T(8,128)} %fusion.191, f32[2,512]{1,0:T(2,128)S(1)} %get-tuple-element.503, f32[2,512]{1,0:T(2,128)S(1)} %get-tuple-element.500, ...), kind=kLoop, calls=%fused_computation.38.clone.1 | loop fusion | flops 37748736 | bytes 62943232 | tf_op jit(solution)/shard_map/while/body/eval_jaxpr/convert_element_type | solution.py:118
  854.1 21.3 %multiply_reduce_fusion.7 = (f32[2,512]{1,0:T(2,128)S(1)}, f32[2,512]{1,0:T(2,128)S(1)}, f32[2,512,3072]{2,1,0:T(8,128)}) fusion(f32[2,512,3072]{2,1,0:T(8,128)} %fusion.191, f32[2,512]{1,0:T(2,128)S(1)} %get-tuple-element.500, f32[3072]{0:T(1024)S(1)} %bitcast.206, f32[2,512,3072]{2,1,0:T(8,128)} %fusion.192, f32[2,512]{1,0:T(2,128)S(1)} %get-tuple-element.501, ...), kind=kOutput, calls=%fused_computation.39.clone.1 | convolution fusion | flops 434108416 | bytes 51409408 | tf_op jit(solution)/shard_map/while/body/eval_jaxpr/bhe,lhe->hbl/dot_general | solution.py:111
  875.5 18.3 %multiply_convert_fusion.4 = (bf16[2,512,3072]{2,1,0:T(8,128)(2,1)S(1)}, bf16[2,512,3072]{2,1,0:T(8,128)(2,1)S(1)}) fusion(f32[2,512,3072]{2,1,0:T(8,128)} %get-tuple-element.502, f32[2,512,3072]{2,1,0:T(8,128)} %fusion.191, f32[2,512]{1,0:T(2,128)S(1)} %get-tuple-element.503, f32[2,512]{1,0:T(2,128)S(1)} %get-tuple-element.500, ...), kind=kLoop, calls=%fused_computation.38.clone.1 | loop fusion | flops 37748736 | bytes 62943232 | tf_op jit(solution)/shard_map/while/body/eval_jaxpr/convert_element_type | solution.py:118
  950.9 20.6 %multiply_reduce_fusion.7 = (f32[2,512]{1,0:T(2,128)S(1)}, f32[2,512]{1,0:T(2,128)S(1)}, f32[2,512,3072]{2,1,0:T(8,128)}) fusion(f32[2,512,3072]{2,1,0:T(8,128)} %fusion.191, f32[2,512]{1,0:T(2,128)S(1)} %get-tuple-element.500, f32[3072]{0:T(1024)S(1)} %bitcast.206, f32[2,512,3072]{2,1,0:T(8,128)} %fusion.192, f32[2,512]{1,0:T(2,128)S(1)} %get-tuple-element.501, ...), kind=kOutput, calls=%fused_computation.39.clone.1 | convolution fusion | flops 434108416 | bytes 51409408 | tf_op jit(solution)/shard_map/while/body/eval_jaxpr/bhe,lhe->hbl/dot_general | solution.py:111
  971.5 18.5 %multiply_convert_fusion.4 = (bf16[2,512,3072]{2,1,0:T(8,128)(2,1)S(1)}, bf16[2,512,3072]{2,1,0:T(8,128)(2,1)S(1)}) fusion(f32[2,512,3072]{2,1,0:T(8,128)} %get-tuple-element.502, f32[2,512,3072]{2,1,0:T(8,128)} %fusion.191, f32[2,512]{1,0:T(2,128)S(1)} %get-tuple-element.503, f32[2,512]{1,0:T(2,128)S(1)} %get-tuple-element.500, ...), kind=kLoop, calls=%fused_computation.38.clone.1 | loop fusion | flops 37748736 | bytes 62943232 | tf_op jit(solution)/shard_map/while/body/eval_jaxpr/convert_element_type | solution.py:118
  1047.2 20.5 %multiply_reduce_fusion.7 = (f32[2,512]{1,0:T(2,128)S(1)}, f32[2,512]{1,0:T(2,128)S(1)}, f32[2,512,3072]{2,1,0:T(8,128)}) fusion(f32[2,512,3072]{2,1,0:T(8,128)} %fusion.191, f32[2,512]{1,0:T(2,128)S(1)} %get-tuple-element.500, f32[3072]{0:T(1024)S(1)} %bitcast.206, f32[2,512,3072]{2,1,0:T(8,128)} %fusion.192, f32[2,512]{1,0:T(2,128)S(1)} %get-tuple-element.501, ...), kind=kOutput, calls=%fused_computation.39.clone.1 | convolution fusion | flops 434108416 | bytes 51409408 | tf_op jit(solution)/shard_map/while/body/eval_jaxpr/bhe,lhe->hbl/dot_general | solution.py:111
  1067.7 17.9 %multiply_convert_fusion.4 = (bf16[2,512,3072]{2,1,0:T(8,128)(2,1)S(1)}, bf16[2,512,3072]{2,1,0:T(8,128)(2,1)S(1)}) fusion(f32[2,512,3072]{2,1,0:T(8,128)} %get-tuple-element.502, f32[2,512,3072]{2,1,0:T(8,128)} %fusion.191, f32[2,512]{1,0:T(2,128)S(1)} %get-tuple-element.503, f32[2,512]{1,0:T(2,128)S(1)} %get-tuple-element.500, ...), kind=kLoop, calls=%fused_computation.38.clone.1 | loop fusion | flops 37748736 | bytes 62943232 | tf_op jit(solution)/shard_map/while/body/eval_jaxpr/convert_element_type | solution.py:118
  1142.5 20.0 %multiply_reduce_fusion.7 = (f32[2,512]{1,0:T(2,128)S(1)}, f32[2,512]{1,0:T(2,128)S(1)}, f32[2,512,3072]{2,1,0:T(8,128)}) fusion(f32[2,512,3072]{2,1,0:T(8,128)} %fusion.191, f32[2,512]{1,0:T(2,128)S(1)} %get-tuple-element.500, f32[3072]{0:T(1024)S(1)} %bitcast.206, f32[2,512,3072]{2,1,0:T(8,128)} %fusion.192, f32[2,512]{1,0:T(2,128)S(1)} %get-tuple-element.501, ...), kind=kOutput, calls=%fused_computation.39.clone.1 | convolution fusion | flops 434108416 | bytes 51409408 | tf_op jit(solution)/shard_map/while/body/eval_jaxpr/bhe,lhe->hbl/dot_general | solution.py:111
  1162.5 17.9 %multiply_convert_fusion.4 = (bf16[2,512,3072]{2,1,0:T(8,128)(2,1)S(1)}, bf16[2,512,3072]{2,1,0:T(8,128)(2,1)S(1)}) fusion(f32[2,512,3072]{2,1,0:T(8,128)} %get-tuple-element.502, f32[2,512,3072]{2,1,0:T(8,128)} %fusion.191, f32[2,512]{1,0:T(2,128)S(1)} %get-tuple-element.503, f32[2,512]{1,0:T(2,128)S(1)} %get-tuple-element.500, ...), kind=kLoop, calls=%fused_computation.38.clone.1 | loop fusion | flops 37748736 | bytes 62943232 | tf_op jit(solution)/shard_map/while/body/eval_jaxpr/convert_element_type | solution.py:118
  1237.3 20.0 %multiply_reduce_fusion.7 = (f32[2,512]{1,0:T(2,128)S(1)}, f32[2,512]{1,0:T(2,128)S(1)}, f32[2,512,3072]{2,1,0:T(8,128)}) fusion(f32[2,512,3072]{2,1,0:T(8,128)} %fusion.191, f32[2,512]{1,0:T(2,128)S(1)} %get-tuple-element.500, f32[3072]{0:T(1024)S(1)} %bitcast.206, f32[2,512,3072]{2,1,0:T(8,128)} %fusion.192, f32[2,512]{1,0:T(2,128)S(1)} %get-tuple-element.501, ...), kind=kOutput, calls=%fused_computation.39.clone.1 | convolution fusion | flops 434108416 | bytes 51409408 | tf_op jit(solution)/shard_map/while/body/eval_jaxpr/bhe,lhe->hbl/dot_general | solution.py:111
  1257.3 17.9 %multiply_convert_fusion.4 = (bf16[2,512,3072]{2,1,0:T(8,128)(2,1)S(1)}, bf16[2,512,3072]{2,1,0:T(8,128)(2,1)S(1)}) fusion(f32[2,512,3072]{2,1,0:T(8,128)} %get-tuple-element.502, f32[2,512,3072]{2,1,0:T(8,128)} %fusion.191, f32[2,512]{1,0:T(2,128)S(1)} %get-tuple-element.503, f32[2,512]{1,0:T(2,128)S(1)} %get-tuple-element.500, ...), kind=kLoop, calls=%fused_computation.38.clone.1 | loop fusion | flops 37748736 | bytes 62943232 | tf_op jit(solution)/shard_map/while/body/eval_jaxpr/convert_element_type | solution.py:118
  1332.6 74.6 %all_to_all.63 = bf16[3072,3,1,256]{3,1,2,0:T(4,128)(2,1)S(1)} all-to-all(bf16[3072,3,1,256]{3,1,2,0:T(4,128)(2,1)} %copy.107), channel_id=1, replica_groups=mesh['dp'=8,'seq'=4] {'seq'}, dimensions={0} | all-to-all | bytes 9437184 | tf_op jit(solution)/shard_map/all_to_all | solution.py:267
  1435.5 115.5 %reduce-scatter.13.cloned.1.call-done = bf16[128,3072]{1,0:T(8,128)(2,1)} async-done(((bf16[1024,3072]{1,0:T(8,128)(2,1)}), bf16[128,3072]{1,0:T(8,128)(2,1)}) %reduce-scatter.13.cloned.1.call-update) | async-done | bytes 786448
  1560.8 35.3 %all-reduce.9 = (bf16[1024]{0:T(1024)(128)(2,1)S(1)}, bf16[1024]{0:T(1024)(128)(2,1)S(1)}, bf16[1024]{0:T(1024)(128)(2,1)S(1)}, bf16[1024]{0:T(1024)(128)(2,1)S(...) all-reduce(bf16[1024]{0:T(1024)(128)(2,1)S(1)} %get-tuple-element.2, ...), channel_id=4, replica_groups=mesh['dp'=8,'seq'=4] {'dp'}, use_global_device_ids=true, to_apply=%region_21.22.clone | all-reduce | flops 12288 | bytes 49152
  1643.9 17.2 %reduce_sum.230 = bf16[128,3072]{0,1:T(8,128)(2,1)} reduce(bf16[4,128,3072]{1,0,2:T(4,128)(2,1)S(1)} %reshape.219, bf16[]{:T(256)} %constant.59.clone.1), dimensions={0}, to_apply=%region_19.20 | reduce | flops 1179648 | bytes 3932162 | tf_op jit(solution)/shard_map/reduce_sum | solution.py:331
  (424 shorter events, 809.1 us)
Async XLA Ops:
  7.2 104.8 %all-gather.16.cloned.1.call-start = ((), (), s32[]{:S(2)}) async-start(), calls=%async_computation.8 | async-start | bytes 7077888 | tf_op jit(solution)/shard_map/all_gather | solution.py:170
  7.9 573.5 %all-gather.18.cloned.1.call-start = ((), (), s32[]{:S(2)}) async-start(), calls=%async_computation.9 | async-start | bytes 2359296 | tf_op jit(solution)/shard_map/all_gather | solution.py:173
  8.7 577.7 %all-gather.20.cloned.1.call-start = ((), (), s32[]{:S(2)}) async-start(), calls=%async_computation.10 | async-start | bytes 9437184 | tf_op jit(solution)/shard_map/all_gather | solution.py:177
  136.0 60.0 %all-to-all-start = ((bf16[768,3,4,256]{3,0,1,2:T(8,128)(2,1)}), bf16[768,3,4,256]{3,0,1,2:T(8,128)(2,1)}, u32[]{:S(2)}, u32[]{:S(2)}) async-start(bf16[768,3,4,256]{3,0,1,2:T(8,128)(2,1)} %copy.93), calls=%async_computation | async-start | bytes 9437184 | tf_op jit(solution)/shard_map/all_to_all | solution.py:200
  141.2 483.9 %all-gather.22.cloned.1.call-start = ((), (), s32[]{:S(2)}) async-start(), calls=%async_computation.11 | async-start | bytes 9437184 | tf_op jit(solution)/shard_map/all_gather | solution.py:179
  394.0 28.4 %copy-start.1 = (bf16[3072,4,64]{0,2,1:T(8,128)(2,1)}, bf16[3072,4,64]{0,2,1:T(8,128)(2,1)S(1)}, u32[]{:S(2)}) copy-start(bf16[3072,4,64]{0,2,1:T(8,128)(2,1)S(1)} %get-tuple-element.587) | copy-start | bytes 4718596
  394.0 28.4 %copy-start.10 = (f32[1,3072]{1,0:T(1,128)}, f32[1,3072]{1,0:T(1,128)S(1)}, u32[]{:S(2)}) copy-start(f32[1,3072]{1,0:T(1,128)S(1)} %get-tuple-element.606) | copy-start | bytes 36868
  394.0 28.4 %copy-start.15 = (f32[6,4,512]{2,1,0:T(4,128)}, f32[6,4,512]{2,1,0:T(4,128)S(1)}, u32[]{:S(2)}) copy-start(f32[6,4,512]{2,1,0:T(4,128)S(1)} %get-tuple-element.540) | copy-start | bytes 147460
  423.0 23.0 %copy-start.26 = (bf16[128]{0:T(256)(128)(2,1)S(1)}, bf16[128]{0:T(256)(128)(2,1)}, u32[]{:S(2)}) copy-start(bf16[128]{0:T(256)(128)(2,1)} %param.26) | copy-start | bytes 772
  423.0 40.4 %copy-start.27 = (bf16[128]{0:T(256)(128)(2,1)S(1)}, bf16[128]{0:T(256)(128)(2,1)}, u32[]{:S(2)}) copy-start(bf16[128]{0:T(256)(128)(2,1)} %param.27) | copy-start | bytes 772
  423.0 57.4 %copy-start.28 = (bf16[128]{0:T(256)(128)(2,1)S(1)}, bf16[128]{0:T(256)(128)(2,1)}, u32[]{:S(2)}) copy-start(bf16[128]{0:T(256)(128)(2,1)} %param.28) | copy-start | bytes 772
  423.0 74.8 %copy-start.25 = (bf16[512]{0:T(512)(128)(2,1)S(1)}, bf16[512]{0:T(512)(128)(2,1)}, u32[]{:S(2)}) copy-start(bf16[512]{0:T(512)(128)(2,1)} %param.30) | copy-start | bytes 3076
  423.0 100.8 %copy-start.29 = (bf16[128]{0:T(256)(128)(2,1)S(1)}, bf16[128]{0:T(256)(128)(2,1)}, u32[]{:S(2)}) copy-start(bf16[128]{0:T(256)(128)(2,1)} %param.32) | copy-start | bytes 772
  423.0 117.0 %copy-start.30 = (bf16[128]{0:T(256)(128)(2,1)S(1)}, bf16[128]{0:T(256)(128)(2,1)}, u32[]{:S(2)}) copy-start(bf16[128]{0:T(256)(128)(2,1)} %param.33) | copy-start | bytes 772
  423.0 135.1 %copy-start.31 = (bf16[128]{0:T(256)(128)(2,1)S(1)}, bf16[128]{0:T(256)(128)(2,1)}, u32[]{:S(2)}) copy-start(bf16[128]{0:T(256)(128)(2,1)} %param.34) | copy-start | bytes 772
  441.6 132.7 %all-to-all-start.1 = ((bf16[4,2,98304]{2,1,0:T(2,128)(2,1)}), bf16[4,2,98304]{2,1,0:T(2,128)(2,1)}, u32[]{:S(2)}, u32[]{:S(2)}) async-start(bf16[4,2,98304]{2,1,0:T(2,128)(2,1)} %reshape.260), calls=%async_computation.1 | async-start | bytes 3145728 | tf_op jit(solution)/shard_map/all_to_all | solution.py:207
  445.9 988.9 %reduce-scatter.7.cloned.1.call-start = ((), (), s32[]{:S(2)}) async-start(), calls=%async_computation.12 | async-start | bytes 2359296 | tf_op jit(solution)/shard_map/reduce_scatter | solution.py:299
  642.3 40.6 %copy-start.18 = (f32[768]{0:T(1024)}, f32[768]{0:T(1024)S(1)}, u32[]{:S(2)}) copy-start(f32[768]{0:T(1024)S(1)} %negate_multiply_fusion.2) | copy-start | bytes 9220
  677.9 17.5 %copy-start.16 = (f32[768]{0:T(1024)}, f32[768]{0:T(1024)S(1)}, u32[]{:S(2)}) copy-start(f32[768]{0:T(1024)S(1)} %negate_multiply_fusion.1) | copy-start | bytes 9220
  682.9 752.0 %reduce-scatter.11.cloned.1.call-start = ((), (), s32[]{:S(2)}) async-start(), calls=%async_computation.14 | async-start | bytes 9437184 | tf_op jit(solution)/shard_map/reduce_scatter | solution.py:317
  703.6 24.5 %all-to-all-start.2 = ((bf16[768,4,256]{0,2,1:T(8,128)(2,1)}), bf16[768,4,256]{0,2,1:T(8,128)(2,1)}, u32[]{:S(2)}, u32[]{:S(2)}) async-start(bf16[768,4,256]{0,2,1:T(8,128)(2,1)} %bitcast.210), calls=%async_computation.2 | async-start | bytes 3145728 | tf_op jit(solution)/shard_map/all_to_all | solution.py:246
  708.0 726.9 %reduce-scatter.9.cloned.1.call-start = ((), (), s32[]{:S(2)}) async-start(), calls=%async_computation.13 | async-start | bytes 9437184 | tf_op jit(solution)/shard_map/reduce_scatter | solution.py:311
  720.6 830.4 %reduce-scatter.13.cloned.1.call-start = ((), (), s32[]{:S(2)}) async-start(), calls=%async_computation.16 | async-start | bytes 7077888
  799.0 15.6 slice-start.3
  990.0 15.6 slice-start.3
  1275.2 15.6 slice-start.3
  1434.7 118.6 %copy-start.7 = (bf16[768,1024]{1,0:T(8,128)(2,1)S(1)}, bf16[768,1024]{1,0:T(8,128)(2,1)}, u32[]{:S(2)}) copy-start(bf16[768,1024]{1,0:T(8,128)(2,1)} %param.35) | copy-start | bytes 4718596
  1434.7 118.9 %copy-start.33 = (u32[32]{0:T(128)S(1)}, u32[32]{0:T(128)}, u32[]{:S(2)}) copy-start(u32[32]{0:T(128)} %constant.126) | copy-start | bytes 388
  1434.7 121.1 %copy-start.19 = (f32[768]{0:T(1024)S(1)}, f32[768]{0:T(1024)}, u32[]{:S(2)}) copy-start(f32[768]{0:T(1024)} %copy-done.18) | copy-start | bytes 9220
  1434.7 183.1 %all-reduce.14.cloned.1.call-start = ((), (), s32[]{:S(2)}) async-start(), calls=%async_computation.17 | async-start | bytes 4718592 | tf_op jit(solution)/shard_map/psum | solution.py:334
  1434.9 123.2 %copy-start.17 = (f32[768]{0:T(1024)S(1)}, f32[768]{0:T(1024)}, u32[]{:S(2)}) copy-start(f32[768]{0:T(1024)} %copy-done.16) | copy-start | bytes 9220
  1435.5 204.6 %all-gather.24.cloned.1.call-start = ((), (), s32[]{:S(2)}) async-start(), calls=%async_computation.15 | async-start | bytes 3932160 | tf_op jit(solution)/shard_map/all_gather | solution.py:331
  (61 other events, 452.6 us)
Sparse Core Ops, SparseCore 0:
  10.2 101.7 all-gather.15
  114.1 47.4 all-gather.17
  163.8 123.4 all-gather.19
  289.2 123.1 all-gather.21
  683.0 66.9 reduce-scatter.6
  753.5 148.0 reduce-scatter.10
  905.6 148.0 reduce-scatter.8
  1434.8 116.1 reduce-scatter.12
  1553.6 55.4 all-reduce.13
  1611.0 29.0 all-gather.23
